TPU v7x, 32 devices: a whole 2x2x4 slice. The times are simulated.
32 devices in a mesh: ctx: 2 (over x), fsdp: 16 (over z, y, core).
Axes of the slice: x: 2, y: 2, z: 4, core: 2. Of those that a mesh axis runs over, the one named last changes fastest.
Arguments:
- tokens_in: bfloat16 [2, 16, 512, 768], P(None, None, ('ctx', 'fsdp')), may hold values from -6 to 6
- out_grad: bfloat16 [2, 16, 512, 768], P(None, None, ('ctx', 'fsdp')), may hold values from -6 to 6
- seq_lengths: int32 [2, 16], replicated, may hold values from 257 to 512, as said below
- order: int32 [2, 16], replicated, may hold values from 0 to 15, as said below
- w_qkv: bfloat16 [768, 2304], P('fsdp'), may hold values from -0.21875 to 0.21875
- bias_q: bfloat16 [768], P('fsdp'), may hold values from -3 to 3
- bias_v: bfloat16 [768], P('fsdp'), may hold values from -3 to 3
- w_out: bfloat16 [768, 768], P('fsdp'), may hold values from -0.875 to 0.875
- bias_out: bfloat16 [768], P('fsdp'), may hold values from -3 to 3
- ln1_gain: bfloat16 [768], P('fsdp'), may hold values from 0.5 to 1.5
- ln1_bias: bfloat16 [768], P('fsdp'), may hold values from -2 to 2
- w_gate_up: bfloat16 [768, 6144], P('fsdp'), may hold values from -0.21875 to 0.21875
- w_down: bfloat16 [3072, 768], P('fsdp'), may hold values from -0.21875 to 0.21875
- bias_down: bfloat16 [768], P('fsdp'), may hold values from -3 to 3
- ln2_gain: bfloat16 [768], P('fsdp'), may hold values from 0.5 to 1.5
- ln2_bias: bfloat16 [768], P('fsdp'), may hold values from -2 to 2
Outputs:
- output: bfloat16 [2, 16, 512, 768], P(None, None, ('ctx', 'fsdp'))
- input_grad: bfloat16 [2, 16, 512, 768], P(None, None, ('ctx', 'fsdp'))
- grad_w_qkv: float32 [768, 2304], P('fsdp')
- grad_bias_q: float32 [768], P('fsdp')
- grad_bias_v: float32 [768], P('fsdp')
- grad_w_out: float32 [768, 768], P('fsdp')
- grad_bias_out: float32 [768], P('fsdp')
- grad_ln1_gain: float32 [768], P('fsdp')
- grad_ln1_bias: float32 [768], P('fsdp')
- grad_w_gate_up: float32 [768, 6144], P('fsdp')
- grad_w_down: float32 [3072, 768], P('fsdp')
- grad_bias_down: float32 [768], P('fsdp')
- grad_ln2_gain: float32 [768], P('fsdp')
- grad_ln2_bias: float32 [768], P('fsdp')
Inputs may be any that keep to these rules, and one draw needn't show every extreme that they name: `seq_lengths`: a sequence's real tokens fill its slots 0 to length - 1; in each micro-batch some sequence fills all 512 slots. `order`: each row is a permutation of the micro-batch's sequences.
All inputs are finite; a program needn't handle non-finite values.
Results may differ from a plain program's by a relative error of at most 0.015.
Values may be sent and summed in bfloat16 or wider, within the bound.
A program may use at most 120 MiB of HBM per device.

v0:
```python
import functools
import math

import jax
import jax.numpy as jnp
from jax import lax
from jax.experimental import pallas as pl
from jax.experimental.pallas import tpu as pltpu
from jax.sharding import PartitionSpec as P

D = 768
HEADS = 12
HEAD_DIM = 64
FF = 3072
M = 2
EPSILON = 1e-12
NEGATIVE = -1e30
MESH = pl.DeviceIdType.MESH
BF = jnp.bfloat16
F32 = jnp.float32
LOG2E = math.log2(math.e)
VMEM_LIMIT = 62 << 20


def slope_list(head_count):

    def powers(number):
        anchor = 2.0 ** (-(2.0 ** (-(math.log2(number) - 3))))
        return [anchor ** (power_index + 1) for power_index in range(number)]

    closest = 2 ** int(math.floor(math.log2(head_count)))
    return powers(closest) + powers(2 * closest)[0::2][: head_count - closest]


def layer_norm(inputs, gain_row, offset_row):
    centre = inputs - jnp.mean(inputs, axis=-1, keepdims=True)
    spread = jnp.mean(centre * centre, axis=-1, keepdims=True)
    return centre * lax.rsqrt(spread + EPSILON) * gain_row + offset_row


def gated_unit(gate_up):
    return jax.nn.gelu(gate_up[:, :FF], approximate=False) * gate_up[:, FF:]


def rows_product(former, latter):
    return lax.dot_general(
        former, latter, (((0,), (0,)), ((), ())), preferred_element_type=jnp.float32
    )


def by_transpose(former, latter):
    return lax.dot_general(
        former, latter, (((1,), (1,)), ((), ())), preferred_element_type=jnp.float32
    )


def plain_product(former, latter):
    return jnp.dot(former, latter, preferred_element_type=jnp.float32)


def masked_scores(heads_q, heads_k, position, key_place, length, slopes):
    raw_scores = (
        jnp.einsum("qhd,khd->hqk", heads_q, heads_k, preferred_element_type=jnp.float32) * 0.125
    )
    distance = jnp.abs(position[:, None] - key_place[None, :]).astype(jnp.float32)
    raw_scores = raw_scores - slopes[:, None, None] * distance[None]
    return jnp.where((key_place < length)[None, None, :], raw_scores, NEGATIVE)


def fetch_weights(shards):
    return (
        lax.all_gather(shards[0], "fsdp", axis=0, tiled=True),
        lax.all_gather(shards[1], "fsdp", axis=0, tiled=True),
        lax.all_gather(shards[2], "fsdp", axis=0, tiled=True),
        lax.all_gather(shards[3], "fsdp", axis=0, tiled=True),
        lax.all_gather(shards[4], "fsdp", axis=0, tiled=True),
        lax.all_gather(shards[5], "fsdp", axis=0, tiled=True),
        lax.all_gather(shards[6], "fsdp", axis=0, tiled=True),
        lax.all_gather(shards[7], "fsdp", axis=0, tiled=True),
        lax.all_gather(shards[8], "fsdp", axis=0, tiled=True),
        lax.all_gather(shards[9], "fsdp", axis=0, tiled=True),
        lax.all_gather(shards[10], "fsdp", axis=0, tiled=True),
        lax.all_gather(shards[11], "fsdp", axis=0, tiled=True),
    )


def reduce_grads(grad_terms):
    shard_sums = (
        lax.psum_scatter(grad_terms[0], "fsdp", scatter_dimension=0, tiled=True),
        lax.psum_scatter(grad_terms[1], "fsdp", scatter_dimension=0, tiled=True),
        lax.psum_scatter(grad_terms[2], "fsdp", scatter_dimension=0, tiled=True),
        lax.psum_scatter(grad_terms[3], "fsdp", scatter_dimension=0, tiled=True),
        lax.psum_scatter(grad_terms[4], "fsdp", scatter_dimension=0, tiled=True),
        lax.psum_scatter(grad_terms[5], "fsdp", scatter_dimension=0, tiled=True),
        lax.psum_scatter(grad_terms[6], "fsdp", scatter_dimension=0, tiled=True),
        lax.psum_scatter(grad_terms[7], "fsdp", scatter_dimension=0, tiled=True),
        lax.psum_scatter(grad_terms[8], "fsdp", scatter_dimension=0, tiled=True),
        lax.psum_scatter(grad_terms[9], "fsdp", scatter_dimension=0, tiled=True),
        lax.psum_scatter(grad_terms[10], "fsdp", scatter_dimension=0, tiled=True),
        lax.psum_scatter(grad_terms[11], "fsdp", scatter_dimension=0, tiled=True),
    )
    return (
        lax.psum(shard_sums[0].astype(jnp.bfloat16), "ctx").astype(jnp.float32),
        lax.psum(shard_sums[1].astype(jnp.bfloat16), "ctx").astype(jnp.float32),
        lax.psum(shard_sums[2].astype(jnp.bfloat16), "ctx").astype(jnp.float32),
        lax.psum(shard_sums[3].astype(jnp.bfloat16), "ctx").astype(jnp.float32),
        lax.psum(shard_sums[4].astype(jnp.bfloat16), "ctx").astype(jnp.float32),
        lax.psum(shard_sums[5].astype(jnp.bfloat16), "ctx").astype(jnp.float32),
        lax.psum(shard_sums[6].astype(jnp.bfloat16), "ctx").astype(jnp.float32),
        lax.psum(shard_sums[7].astype(jnp.bfloat16), "ctx").astype(jnp.float32),
        lax.psum(shard_sums[8].astype(jnp.bfloat16), "ctx").astype(jnp.float32),
        lax.psum(shard_sums[9].astype(jnp.bfloat16), "ctx").astype(jnp.float32),
        lax.psum(shard_sums[10].astype(jnp.bfloat16), "ctx").astype(jnp.float32),
        lax.psum(shard_sums[11].astype(jnp.bfloat16), "ctx").astype(jnp.float32),
    )


def per_device_plain(
    tokens_in,
    out_grad,
    seq_lengths,
    order,
    w_qkv,
    bias_q,
    bias_v,
    w_out,
    bias_out,
    ln1_gain,
    ln1_bias,
    w_gate_up,
    w_down,
    bias_down,
    ln2_gain,
    ln2_bias,
):
    shards = (
        w_qkv,
        bias_q,
        bias_v,
        w_out,
        bias_out,
        ln1_gain,
        ln1_bias,
        w_gate_up,
        w_down,
        bias_down,
        ln2_gain,
        ln2_bias,
    )
    group_index = lax.axis_index("fsdp")
    ctx_index = lax.axis_index("ctx")
    dealt_tokens = jnp.take_along_axis(tokens_in, order[:, :, None, None], axis=1)
    tokens_grp, grads_grp = (
        lax.all_to_all(dealt_tokens, "fsdp", split_axis=1, concat_axis=2, tiled=True),
        lax.all_to_all(out_grad, "fsdp", split_axis=1, concat_axis=2, tiled=True),
    )
    dealt_lengths = jnp.take_along_axis(seq_lengths, order, axis=1)
    local_rows = tokens_grp.shape[2]
    key_place = jnp.arange(local_rows * lax.axis_size("ctx"))
    position = ctx_index * local_rows + jnp.arange(local_rows)
    slopes = jnp.array(slope_list(HEADS), jnp.float32)
    output_list = []
    input_list = []
    running = None
    for micro_batch in range(M):
        weights = fetch_weights(shards)
        (
            full_qkv,
            full_bias_q,
            full_bias_v,
            full_out,
            full_bias_out,
            full_ln1_gain,
            full_ln1_bias,
            full_gate_up,
            full_down,
            full_bias_down,
            full_ln2_gain,
            full_ln2_bias,
        ) = weights
        tokens = tokens_grp[micro_batch, 0]
        cotangent = grads_grp[micro_batch, 0]
        length = lax.dynamic_index_in_dim(
            dealt_lengths[micro_batch], group_index, 0, keepdims=False
        )
        valid_rows = position < length
        projected = plain_product(tokens, full_qkv)
        queries = (projected[:, :D] + full_bias_q.astype(jnp.float32)).astype(jnp.bfloat16)
        key_rows = projected[:, D : 2 * D].astype(jnp.bfloat16)
        values = (projected[:, 2 * D :] + full_bias_v.astype(jnp.float32)).astype(jnp.bfloat16)
        keys_all, values_all = (
            lax.all_gather(key_rows, "ctx", axis=0, tiled=True),
            lax.all_gather(values, "ctx", axis=0, tiled=True),
        )
        heads_q = queries.reshape(local_rows, HEADS, HEAD_DIM)
        heads_k = keys_all.reshape(-1, HEADS, HEAD_DIM)
        heads_v = values_all.reshape(-1, HEADS, HEAD_DIM)
        scores = masked_scores(heads_q, heads_k, position, key_place, length, slopes)
        row_max = jnp.max(scores, axis=-1, keepdims=True)
        exp_terms = jnp.exp(scores - row_max)
        row_total = jnp.sum(exp_terms, axis=-1, keepdims=True)
        log_total = row_max + jnp.log(row_total)
        attn_probs = (exp_terms / row_total).astype(jnp.bfloat16)
        context = (
            jnp.einsum("hqk,khd->qhd", attn_probs, heads_v, preferred_element_type=jnp.float32)
            .reshape(local_rows, D)
            .astype(jnp.bfloat16)
        )
        attn_out = plain_product(context, full_out) + full_bias_out.astype(jnp.float32)
        first_sum = tokens.astype(jnp.float32) + attn_out
        normed_one, norm_one_pull = jax.vjp(
            layer_norm,
            first_sum,
            full_ln1_gain.astype(jnp.float32),
            full_ln1_bias.astype(jnp.float32),
        )
        normed_low = normed_one.astype(jnp.bfloat16)
        gate_up = plain_product(normed_low, full_gate_up)
        hidden, gated_pull = jax.vjp(gated_unit, gate_up)
        hidden_low = hidden.astype(jnp.bfloat16)
        branch = plain_product(hidden_low, full_down) + full_bias_down.astype(jnp.float32)
        result, norm_two_pull = jax.vjp(
            layer_norm,
            normed_one + branch,
            full_ln2_gain.astype(jnp.float32),
            full_ln2_bias.astype(jnp.float32),
        )
        output_list.append(jnp.where(valid_rows[:, None], result, 0.0).astype(jnp.bfloat16))
        grad_result = jnp.where(valid_rows[:, None], cotangent.astype(jnp.float32), 0.0)
        grad_second, grad_ln2_gain, grad_ln2_bias = norm_two_pull(grad_result)
        grad_branch = grad_second.astype(jnp.bfloat16)
        grad_bias_down = jnp.sum(grad_branch.astype(jnp.float32), axis=0)
        grad_w_down = rows_product(hidden_low, grad_branch)
        grad_hidden = by_transpose(grad_branch, full_down)
        (grad_gate_up,) = gated_pull(grad_hidden)
        grad_gate_low = grad_gate_up.astype(jnp.bfloat16)
        grad_w_gate_up = rows_product(normed_low, grad_gate_low)
        grad_normed = grad_second + by_transpose(grad_gate_low, full_gate_up)
        grad_first, grad_ln1_gain, grad_ln1_bias = norm_one_pull(grad_normed)
        grad_attn = grad_first.astype(jnp.bfloat16)
        grad_bias_out = jnp.sum(grad_attn.astype(jnp.float32), axis=0)
        grad_w_out = rows_product(context, grad_attn)
        grad_context = (
            by_transpose(grad_attn, full_out)
            .astype(jnp.bfloat16)
            .reshape(local_rows, HEADS, HEAD_DIM)
        )
        scores = masked_scores(heads_q, heads_k, position, key_place, length, slopes)
        attn_exact = jnp.exp(scores - log_total)
        grad_values_term = jnp.einsum(
            "hqk,qhd->khd",
            attn_exact.astype(jnp.bfloat16),
            grad_context,
            preferred_element_type=jnp.float32,
        )
        grad_probs = jnp.einsum(
            "qhd,khd->hqk", grad_context, heads_v, preferred_element_type=jnp.float32
        )
        grad_scores = (
            attn_exact * (grad_probs - jnp.sum(attn_exact * grad_probs, axis=-1, keepdims=True))
        ).astype(jnp.bfloat16)
        grad_queries = (
            jnp.einsum("hqk,khd->qhd", grad_scores, heads_k, preferred_element_type=jnp.float32)
            * 0.125
        ).reshape(local_rows, D)
        grad_keys_term = (
            jnp.einsum("hqk,qhd->khd", grad_scores, heads_q, preferred_element_type=jnp.float32)
            * 0.125
        )
        grad_keys, grad_values = (
            lax.psum_scatter(
                grad_keys_term.reshape(-1, D).astype(jnp.bfloat16),
                "ctx",
                scatter_dimension=0,
                tiled=True,
            ).astype(jnp.float32),
            lax.psum_scatter(
                grad_values_term.reshape(-1, D).astype(jnp.bfloat16),
                "ctx",
                scatter_dimension=0,
                tiled=True,
            ).astype(jnp.float32),
        )
        grad_qkv = jnp.concatenate(
            [
                grad_queries.astype(jnp.bfloat16),
                grad_keys.astype(jnp.bfloat16),
                grad_values.astype(jnp.bfloat16),
            ],
            axis=1,
        )
        grad_w_qkv = rows_product(tokens, grad_qkv)
        grad_bias_q = jnp.sum(grad_qkv[:, :D].astype(jnp.float32), axis=0)
        grad_bias_v = jnp.sum(grad_qkv[:, 2 * D :].astype(jnp.float32), axis=0)
        grad_tokens = grad_first + by_transpose(grad_qkv, full_qkv)
        input_list.append(grad_tokens.astype(jnp.bfloat16))
        grad_terms = (
            grad_w_qkv,
            grad_bias_q,
            grad_bias_v,
            grad_w_out,
            grad_bias_out,
            grad_ln1_gain,
            grad_ln1_bias,
            grad_w_gate_up,
            grad_w_down,
            grad_bias_down,
            grad_ln2_gain,
            grad_ln2_bias,
        )
        reduced = reduce_grads(grad_terms)
        if micro_batch == 0:
            running = reduced
        else:
            running = tuple((left_sum + right_sum for left_sum, right_sum in zip(running, reduced)))
    output_stack = jnp.stack(output_list, axis=0)[:, None]
    input_stack = jnp.stack(input_list, axis=0)[:, None]
    output, dealt_grads = (
        lax.all_to_all(output_stack, "fsdp", split_axis=2, concat_axis=1, tiled=True),
        lax.all_to_all(input_stack, "fsdp", split_axis=2, concat_axis=1, tiled=True),
    )
    inverse = jnp.argsort(order, axis=1)
    input_grad = jnp.take_along_axis(dealt_grads, inverse[:, :, None, None], axis=1)
    return (
        output,
        input_grad,
        running[0],
        running[1],
        running[2],
        running[3],
        running[4],
        running[5],
        running[6],
        running[7],
        running[8],
        running[9],
        running[10],
        running[11],
    )


PIECES = 16
RING = 4


def whole(p, w=256):
    return [(p, 0, D, w)]


def halves(p, w=128):
    return [(p, 384 * i, 384, w) for i in range(2)]


GATHER_UNITS = sum([whole(p, 384 if p in (6, 10) else 256) for p in range(PIECES)], [])
SCATTER_UNITS = sum([whole(p, 256 if i % 3 else 128) for i, p in enumerate([*range(4, 16), 3, 0, 1, 2])], [])
STAGES = ()
AHEAD = 0
ROW_AT = 4
PLANE_AT = 6
CORE_AT = 8
X_AT = (0, 7)
G_AT = (7, 9)
O_AT = (0, 8)
O_FIRST = True
D_AT = (13, 7)


def mm(a, b):
    return jnp.dot(a, b, preferred_element_type=F32)


def mm_nt(a, b):
    return lax.dot_general(a, b, (((1,), (1,)), ((), ())), preferred_element_type=F32)


def mm_tn(a, b):
    return lax.dot_general(a, b, (((0,), (0,)), ((), ())), preferred_element_type=F32)


def block(i, size):
    if isinstance(i, int):
        return pl.ds(i * size, size)
    return pl.ds(pl.multiple_of(i * size, size), size)


class Place:
    def __init__(self, fsdp):
        self.fsdp = fsdp
        self.total = 2 * fsdp
        self.Z = fsdp // 4
        self.x = lax.axis_index("ctx")
        self.f = lax.axis_index("fsdp")
        self.z = self.f // 4
        self.y = lax.rem(self.f // 2, 2)
        self.c = lax.rem(self.f, 2)
        self.me = self.x * fsdp + self.f
        self.pending = []

    def dev(self, x=None, z=None, y=None, c=None):
        x = self.x if x is None else x
        z = self.z if z is None else z
        y = self.y if y is None else y
        c = self.c if c is None else c
        return (x, z * 4 + y * 2 + c)

    def cols(self, unit):
        p, lo, n, w = unit
        return pl.ds(pl.multiple_of(lo + self.x * w, 128), n - w)

    def give(self, unit):
        p, lo, n, w = unit
        return pl.ds(pl.multiple_of(lo + self.x * (n - w), 128), w)

    def take(self, unit):
        p, lo, n, w = unit
        return pl.ds(pl.multiple_of(lo + (1 - self.x) * (n - w), 128), w)

    def at(self, d):
        return (d // self.fsdp, lax.rem(d, self.fsdp))

    def signal(self):
        sem = pltpu.get_barrier_semaphore()

        @pl.loop(1, self.total)
        def _(k):
            d = lax.rem(self.me + k, self.total)
            pl.semaphore_signal(sem, inc=1, device_id=self.at(d), device_id_type=MESH)

    def wait(self):
        pl.semaphore_wait(pltpu.get_barrier_semaphore(), self.total - 1)

    def go(self, copy, cond=None):
        if cond is None:
            copy.start()
        else:
            pl.when(cond)(copy.start)
        self.pending.append((cond, copy))

    def finish(self):
        for cond, copy in self.pending:
            if cond is None:
                copy.wait_send()
            else:
                pl.when(cond)(copy.wait_send)
        self.pending = []


def remote(src, dst, send, recv, device):
    return pltpu.make_async_remote_copy(
        src_ref=src, dst_ref=dst, send_sem=send, recv_sem=recv, device_id=device, device_id_type=MESH
    )


class Exchange:
    def __init__(self, pc, src, dst, sems, k):
        self.pc, self.src, self.dst = pc, src, dst
        self.send, self.recv, self.local = sems[0].at[k], sems[1].at[k], sems[2].at[k]

    def own(self):
        return pltpu.make_async_copy(self.src.at[self.pc.me], self.dst.at[self.pc.me], self.local)

    def start(self, turn=0, turns=1):
        pc = self.pc
        if turn == 0:
            self.own().start()
        near = [(x, 0, y, c) for x in range(2) for y in range(2) for c in range(2) if x + y + c]
        far = [(x, z, y, c) for x in range(2) for y in range(2) for c in range(2) for z in (2, 3, 1)]
        if turns > 1:
            per = -(-len(far) // (turns - 1))
            picked = far[(turn - 1) * per : turn * per] if turn else near
        else:
            picked = near + far
        for x, z, y, c in picked:
            to = pc.dev(
                x=(1 - pc.x) if x else None,
                y=(1 - pc.y) if y else None,
                c=(1 - pc.c) if c else None,
                z=(None, pc.z + 1 - 2 * lax.rem(pc.z, 2), lax.rem(pc.z + 2, 4), 3 - pc.z)[z],
            )
            d = to[0] * pc.fsdp + to[1]
            remote(self.src.at[d], self.dst.at[pc.me], self.send, self.recv, to).start()

    def whole(self):
        blocks = pl.ds(0, self.pc.total - 1)
        return remote(self.src.at[blocks], self.dst.at[blocks], self.send, self.recv, self.pc.dev(c=1 - self.pc.c))

    def wait(self):
        self.own().wait()
        self.whole().wait_recv()

    def done(self):
        self.whole().wait_send()


class Gather:
    def __init__(self, pc, own, slots, sems):
        self.pc, self.own = pc, own
        self.place = slots
        self.zs, self.zr, self.ys, self.yr, self.xs, self.xr, self.cs, self.cr, self.ls = sems

    @staticmethod
    def sems(Z):
        T = pltpu.SemaphoreType.DMA
        n = len(GATHER_UNITS)
        return [
            T((n, 2 * Z - 2)), T((n, 2 * Z - 2)), T((n, 2 * Z - 1)), T((n,)),
            T((n, 2 * Z - 1)), T((n, 2 * Z - 1)), T((n, 2)), T((n, 2)), T((n,)),
        ]

    def up(self):
        return jnp.minimum(self.pc.z + 1, self.pc.Z - 1)

    def down(self):
        return jnp.maximum(self.pc.z - 1, 0)

    def slots(self, u, z, y, cols):
        return self.place(GATHER_UNITS[u][0], z, y, self.pc.c, cols)

    def cols(self, u):
        return self.pc.cols(GATHER_UNITS[u])

    def mine(self, u):
        pc = self.pc
        p, lo, n, w = GATHER_UNITS[u]
        return pltpu.make_async_copy(self.own(p, pl.ds(lo, n)), self.slots(u, pc.z, pc.y, pl.ds(lo, n)), self.ls.at[u])

    def start(self, u):
        pc = self.pc
        Z = pc.Z
        src = self.own(GATHER_UNITS[u][0], self.cols(u))
        dst = self.slots(u, pc.z, pc.y, self.cols(u))
        self.mine(u).start()
        pc.go(remote(src, dst, self.zs.at[u, 0], self.zr.at[u, 0], pc.dev(z=self.up())), pc.z < Z - 1)
        k = Z - 1
        pc.go(remote(src, dst, self.zs.at[u, k], self.zr.at[u, k], pc.dev(z=self.down())), pc.z > 0)
        pc.go(remote(src, dst, self.ys.at[u, 0], self.yr.at[u], pc.dev(y=1 - pc.y)))

    def hops(self, h):
        pc = self.pc
        Z = pc.Z
        return (
            (jnp.maximum(pc.z - h, 0), pc.z >= h, pc.z < Z - 1, self.up(), h - 1),
            (jnp.minimum(pc.z + h, Z - 1), pc.z + h < Z, pc.z > 0, self.down(), Z + h - 2),
        )

    def hop(self, u, h):
        pc = self.pc
        for z, here, onward, to, k in self.hops(h):
            ref = self.slots(u, z, pc.y, self.cols(u))
            pl.when(here)(remote(ref, ref, self.zs.at[u, k], self.zr.at[u, k], pc.dev(z=to)).wait_recv)
            if h < pc.Z - 1:
                pc.go(
                    remote(ref, ref, self.zs.at[u, k + 1], self.zr.at[u, k + 1], pc.dev(z=to)),
                    jnp.logical_and(here, onward),
                )
            pc.go(remote(ref, ref, self.ys.at[u, 1 + k], self.yr.at[u], pc.dev(y=1 - pc.y)), here)
            if GATHER_UNITS[u][3]:
                ref = self.slots(u, z, pc.y, pc.give(GATHER_UNITS[u]))
                pc.go(remote(ref, ref, self.xs.at[u, k], self.xr.at[u, k], pc.dev(x=1 - pc.x)), here)

    def row(self, u):
        pc = self.pc
        unit = GATHER_UNITS[u]
        ref = self.slots(u, slice(None), 1 - pc.y, self.cols(u))
        remote(ref, ref, self.ys.at[u, 0], self.yr.at[u], pc.dev(y=1 - pc.y)).wait_recv()
        if unit[3]:
            k = 2 * pc.Z - 2
            ref = self.slots(u, slice(None), 1 - pc.y, pc.give(unit))
            pc.go(remote(ref, ref, self.xs.at[u, k], self.xr.at[u, k], pc.dev(x=1 - pc.x)))
        self.mine(u).wait()
        ref = self.slots(u, slice(None), slice(None), self.cols(u))
        pc.go(remote(ref, ref, self.cs.at[u, 0], self.cr.at[u, 0], pc.dev(c=1 - pc.c)))

    def plane(self, u):
        pc = self.pc
        unit = GATHER_UNITS[u]
        if not unit[3]:
            return
        take = pc.take(unit)
        for h in range(1, pc.Z):
            for z, here, onward, to, k in self.hops(h):
                ref = self.slots(u, z, pc.y, take)
                pl.when(here)(remote(ref, ref, self.xs.at[u, k], self.xr.at[u, k], pc.dev(x=1 - pc.x)).wait_recv)
        k = 2 * pc.Z - 2
        ref = self.slots(u, slice(None), 1 - pc.y, take)
        remote(ref, ref, self.xs.at[u, k], self.xr.at[u, k], pc.dev(x=1 - pc.x)).wait_recv()
        ref = self.slots(u, slice(None), slice(None), take)
        pc.go(remote(ref, ref, self.cs.at[u, 1], self.cr.at[u, 1], pc.dev(c=1 - pc.c)))

    def core(self, u):
        pc = self.pc
        parts = [pc.cols(GATHER_UNITS[u])] + ([pc.take(GATHER_UNITS[u])] if GATHER_UNITS[u][3] else [])
        for k, cols in enumerate(parts):
            ref = self.place(GATHER_UNITS[u][0], slice(None), slice(None), 1 - pc.c, cols)
            remote(ref, ref, self.cs.at[u, k], self.cr.at[u, k], pc.dev(c=1 - pc.c)).wait_recv()


class Scatter:
    def __init__(self, pc, terms, get, put, from_c, from_x, from_y, from_z, from_f, sems):
        self.pc, self.terms, self.get, self.put = pc, terms, get, put
        self.from_c, self.from_x, self.from_y, self.from_z, self.from_f = from_c, from_x, from_y, from_z, from_f
        self.cs, self.cr, self.xs, self.xr, self.ys, self.yr, self.zs, self.zr, self.fs, self.fr, self.free = sems
        z = pc.z
        self.inner = jnp.logical_or(z == 1, z == 2)
        self.outer = jnp.logical_not(self.inner)
        self.mate = z + 1 - 2 * lax.rem(z, 2)
        self.far_in = jnp.where(z < 2, 2, 1)
        self.far_out = jnp.where(z < 2, 3, 0)
        self.x_lo, self.y_lo = [], []
        used = {}
        for p, lo, n, w in SCATTER_UNITS:
            a, b = used.get(p, (0, 0))
            self.x_lo.append(a)
            self.y_lo.append(b)
            used[p] = (a + w, b + n - w)

    @staticmethod
    def sems():
        T = pltpu.SemaphoreType.DMA
        n = len(SCATTER_UNITS)
        return [
            T((n,)), T((n,)), T((n,)), T((n,)), T((n,)), T((n,)), T((n, 5)), T((n, 4)), T((n,)), T((n,)),
            pltpu.SemaphoreType.REGULAR((n,)),
        ]

    @staticmethod
    def buffers(Z, rows):
        n = PIECES
        give, win = [0] * n, [0] * n
        for p, lo, k, w in SCATTER_UNITS:
            give[p] += w
            win[p] += k - w
        give, win = max(give), max(win)
        return [
            pltpu.VMEM((RING, Z, 2, rows, D), BF),
            pltpu.VMEM((n, Z, 2, rows, give), BF),
            pltpu.VMEM((n, Z, rows, win), BF),
            pltpu.VMEM((n, 4, rows, win), BF),
            pltpu.VMEM((n, rows, win), BF),
        ]

    def x_at(self, u):
        return pl.ds(self.x_lo[u], SCATTER_UNITS[u][3])

    def y_at(self, u):
        p, lo, n, w = SCATTER_UNITS[u]
        return pl.ds(self.y_lo[u], n - w)

    def add(self, u, z, y, cols, value):
        p = SCATTER_UNITS[u][0]
        c = self.pc.c
        self.put(p, z, y, c, cols, self.get(p, z, y, c, cols) + value)

    def part(self, u, z, y, cols):
        return self.terms(SCATTER_UNITS[u][0], z, y, self.pc.c, cols)

    def start(self, u):
        pc = self.pc
        p, lo, n, w = SCATTER_UNITS[u]
        if u >= RING:
            pl.semaphore_wait(self.free.at[u], 1)
        src = self.terms(p, slice(None), slice(None), 1 - pc.c, pl.ds(lo, n))
        dst = self.from_c.at[u % RING, :, :, :, pl.ds(0, n)]
        pc.go(remote(src, dst, self.cs.at[u], self.cr.at[u], pc.dev(c=1 - pc.c)))

    def core(self, u):
        pc = self.pc
        p, lo, n, w = SCATTER_UNITS[u]
        ref = self.from_c.at[u % RING, :, :, :, pl.ds(0, n)]
        remote(ref, ref, self.cs.at[u], self.cr.at[u], pc.dev(c=1 - pc.c)).wait_recv()
        for z in range(pc.Z):
            for y in range(2):
                self.add(u, z, y, pl.ds(lo, n), self.from_c[u % RING, z, y, :, pl.ds(0, n)])
        if u + RING < len(SCATTER_UNITS):
            pl.semaphore_signal(self.free.at[u + RING], inc=1, device_id=pc.dev(c=1 - pc.c), device_id_type=MESH)
        if w:
            src = self.part(u, slice(None), slice(None), pc.take(SCATTER_UNITS[u]))
            dst = self.from_x.at[p, :, :, :, self.x_at(u)]
            pc.go(remote(src, dst, self.xs.at[u], self.xr.at[u], pc.dev(x=1 - pc.x)))
        else:
            self.across(u)

    def plane(self, u):
        pc = self.pc
        p, lo, n, w = SCATTER_UNITS[u]
        if w:
            ref = self.from_x.at[p, :, :, :, self.x_at(u)]
            remote(ref, ref, self.xs.at[u], self.xr.at[u], pc.dev(x=1 - pc.x)).wait_recv()
            for z in range(pc.Z):
                for y in range(2):
                    self.add(u, z, y, pc.give(SCATTER_UNITS[u]), self.from_x[p, z, y, :, self.x_at(u)])
            self.across(u)

    def across(self, u):
        pc = self.pc
        src = self.part(u, slice(None), 1 - pc.y, pc.cols(SCATTER_UNITS[u]))
        dst = self.from_y.at[SCATTER_UNITS[u][0], :, :, self.y_at(u)]
        pc.go(remote(src, dst, self.ys.at[u], self.yr.at[u], pc.dev(y=1 - pc.y)))

    def z_ref(self, u, k):
        return self.from_z.at[SCATTER_UNITS[u][0], k, :, self.y_at(u)]

    def z_add(self, u, k, z):
        ref = self.z_ref(u, k)
        remote(ref, ref, self.zs.at[u, k], self.zr.at[u, k], self.pc.dev(z=self.mate)).wait_recv()
        value = self.from_z[SCATTER_UNITS[u][0], k, :, self.y_at(u)]
        self.add(u, z, self.pc.y, self.pc.cols(SCATTER_UNITS[u]), value)

    def row(self, u):
        pc = self.pc
        p = SCATTER_UNITS[u][0]
        cols = pc.cols(SCATTER_UNITS[u])
        ref = self.from_y.at[p, :, :, self.y_at(u)]
        remote(ref, ref, self.ys.at[u], self.yr.at[u], pc.dev(y=1 - pc.y)).wait_recv()
        for z in range(pc.Z):
            self.add(u, z, pc.y, cols, self.from_y[p, z, :, self.y_at(u)])
        for k, z in enumerate((self.mate, self.far_in, self.far_out)):
            copy = remote(
                self.part(u, z, pc.y, cols), self.z_ref(u, k), self.zs.at[u, k], self.zr.at[u, k], pc.dev(z=self.mate)
            )
            pc.go(copy, self.outer if k else None)

    def middle(self, u):
        pc = self.pc
        cols = pc.cols(SCATTER_UNITS[u])
        far = ((1, self.far_in), (2, self.far_out))

        @pl.when(self.inner)
        def _():
            for k, z in far:
                self.z_add(u, k, z)

        for k, z in far:
            src = self.part(u, z, pc.y, cols)
            pc.go(remote(src, self.z_ref(u, 3), self.zs.at[u, 2 + k], self.zr.at[u, 3], pc.dev(z=z)), self.inner)

    def f_ref(self, u):
        return self.from_f.at[SCATTER_UNITS[u][0], :, self.y_at(u)]

    def line(self, u):
        pc = self.pc
        for k in (0, 3):
            self.z_add(u, k, pc.z)
        src = self.part(u, pc.z, pc.y, pc.cols(SCATTER_UNITS[u]))
        pc.go(remote(src, self.f_ref(u), self.fs.at[u], self.fr.at[u], pc.dev(x=1 - pc.x)))

    def last(self, u, out):
        pc = self.pc
        unit = p, lo, n, w = SCATTER_UNITS[u]
        ref = self.f_ref(u)
        remote(ref, ref, self.fs.at[u], self.fr.at[u], pc.dev(x=1 - pc.x)).wait_recv()
        at = self.y_lo[u]

        def own(cols):
            return self.get(p, pc.z, pc.y, pc.c, cols).astype(F32)

        if w:
            out[:, pc.give(unit)] = own(pc.give(unit))
            theirs = pl.ds(pl.multiple_of(at + (1 - pc.x) * (n - 2 * w), 128), w)
            out[:, pc.take(unit)] = self.from_f[p, :, theirs].astype(F32)
        if n > 2 * w:
            both = pl.ds(pl.multiple_of(at + pc.x * w, 128), n - 2 * w)
            shared = pl.ds(lo + w, n - 2 * w)
            out[:, shared] = own(shared) + self.from_f[p, :, both].astype(F32)


def row_mean(v):
    return jnp.sum(v, axis=-1, keepdims=True) * (1.0 / D)


BQ, BV, BO, G1, B1, BD, G2, B2 = range(8)


def layer_kernel(
    fsdp, rows,
    order, lengths, slopes, tokens_in, grads_in, *refs,
):
    small_in, (wq_in, wo_in, wg_in, wd_in) = refs[:8], refs[8:12]
    OUT, DX, GQ, GW, GG, GD, SMALLG, *refs = refs[12:]
    (
    wa, wd, raw, outv, xs, gs, small, small_own, smallf, qkv, dist, lse, ctxt, y1, y1b, xhat, rstd, act, slope_up, zed, acc, dfb, tr,
    dxr, sgrad, sparts, gsum, from_c, from_x, from_y, from_z, from_f, *sems,
    ) = refs
    pc = Place(fsdp)
    Z = pc.Z
    L = pc.total * raw.shape[1]
    gsems, ssems, esems, rsem = sems[:9], sems[9:20], sems[20:23], sems[23]
    w_pc = wa.shape[1:]

    def own(p, cols):
        if p < 3:
            return wq_in.at[:, pl.ds(pl.multiple_of(D * p + cols.start, 128), cols.size)]
        if p == 3:
            return wo_in.at[:, cols]
        if p < 12:
            i, j = (p - 4) // 2, (p - 4) % 2
            return wg_in.at[:, pl.ds(pl.multiple_of(FF * j + D * i + cols.start, 128), cols.size)]
        return wd_in.at[pl.ds(rows * (p - 12), rows), cols]

    def slots(p, z, y, c, cols):
        if p < 12:
            return wa.at[p, z, y, c, :, cols]
        return wd.at[z, y, c, p - 12, :, cols]

    def get(p, z, y, c, cols):
        if p < 12:
            return wa[p, z, y, c, :, cols]
        return wd[z, y, c, p - 12, :, cols]

    def put(p, z, y, c, cols, value):
        if p < 12:
            wa[p, z, y, c, :, cols] = value
        else:
            wd[z, y, c, p - 12, :, cols] = value

    def out_of(p):
        if p >= 12:
            return GD.at[pl.ds(rows * (p - 12), rows)]
        if p == 3:
            return GW
        if p < 3:
            return GQ.at[:, pl.ds(D * p, D)]
        i, j = (p - 4) // 2, (p - 4) % 2
        return GG.at[:, pl.ds(FF * j + D * i, D)]

    def w_cols(p, cols):
        return wa[p, :, :, :, :, cols].reshape(D, cols.size)

    def w_all(p):
        return wa[p].reshape(D, D)

    g = Gather(pc, own, slots, gsems)
    sc = Scatter(pc, slots, get, put, from_c, from_x, from_y, from_z, from_f, ssems)
    ex_x = Exchange(pc, outv, xs, esems, 0)
    ex_g = Exchange(pc, grads_in, gs, esems, 1)
    ex_o = Exchange(pc, outv, OUT, esems, 3)
    ex_d = Exchange(pc, raw, dxr, esems, 4)
    ex_s = Exchange(pc, sparts, gsum, esems, 5)
    len_s = lengths[pc.x, order[pc.x, pc.f]]

    def tokens(r):
        n = r.size // 16
        return xs[pl.ds(r.start // 16, n)].reshape(r.size, D)

    def deal():
        @pl.loop(0, pc.total)
        def _(d):
            m = d // fsdp
            outv[d] = raw[m * fsdp + order[m, lax.rem(d, fsdp)]]

    def prepare():
        k = lax.broadcasted_iota(jnp.int32, (L, L), 0)
        q = lax.broadcasted_iota(jnp.int32, (L, L), 1)
        dist[...] = jnp.where(k < len_s, jnp.abs(k - q).astype(F32), -NEGATIVE)

    def place_small():
        for f in range(fsdp):
            smallf[:, pl.ds(f * rows, rows)] = small[f, :, pl.ds(0, rows)]

    def project(p):
        @pl.loop(0, D // 256)
        def _(t):
            cols = block(t, 256)
            r = mm(xs[...].reshape(L, D), w_cols(p, cols))
            if p != 1:
                r = r + smallf[pl.ds(BQ if p == 0 else BV, 1), cols]
            qkv[p, :, cols] = r.astype(BF)

    def attend(j):
        cols = block(j, 128)
        lane = lax.broadcasted_iota(jnp.int32, (L, 128), 1)
        q2, k2 = qkv[0, :, cols], qkv[1, :, cols]
        vt = qkv[2, :, cols].T
        for q in range(L // 256):
            qr = pl.ds(256 * q, 256)
            parts = []
            for s in range(2):
                qm = jnp.where((lane < 64) if s == 0 else (lane >= 64), q2, jnp.zeros_like(q2))
                st = mm_nt(k2, qm[256 * q : 256 * q + 256])
                st = st * (0.125 * LOG2E) - dist[:, qr] * slopes[2 * j + s]
                top = jnp.max(st, axis=0, keepdims=True)
                e = jnp.exp2(st - top)
                total = jnp.sum(e, axis=0, keepdims=True)
                lse[2 * j + s, :, qr] = top + jnp.log2(total)
                pr = (e * (1.0 / total)).astype(BF)
                parts.append(mm(vt[64 * s : 64 * s + 64], pr))
            ctxt[qr, cols] = jnp.concatenate(parts, axis=0).T.astype(BF)

    def first_sum():
        @pl.loop(0, D // 256)
        def _(t):
            cols = block(t, 256)
            acc[:, cols] = mm(ctxt[...], w_cols(3, cols)) + smallf[pl.ds(BO, 1), cols]

    def first_norm():
        @pl.loop(0, L // 64)
        def _(i):
            r = block(i, 64)
            h = acc[r, :] + tokens(r).astype(F32)
            centre = h - row_mean(h)
            rs = lax.rsqrt(row_mean(centre * centre) + EPSILON)
            xh = centre * rs
            xhat[r, :] = xh
            rstd[r, :] = jnp.broadcast_to(rs, (64, 128))
            yy = xh * smallf[pl.ds(G1, 1), :] + smallf[pl.ds(B1, 1), :]
            y1[r, :] = yy
            y1b[r, :] = yy.astype(BF)

        tr[...] = y1b[...].T

    def gated(i):
        for s in range(D // 256):
            gated_part(i, s)

    def gated_part(i, s):
        wc = block(s, 256)
        cols = block(i * 3 + s, 256)
        a = mm(y1b[...], w_cols(4 + 2 * i, wc))
        u = mm(y1b[...], w_cols(5 + 2 * i, wc))
        cdf = 0.5 + 0.5 * lax.erf(a * math.sqrt(0.5))
        pdf = jnp.exp2(a * a * (-0.5 * LOG2E)) * (1.0 / math.sqrt(2.0 * math.pi))
        gelu = a * cdf
        zed[:, cols] = (gelu * u).astype(BF)
        act[:, cols] = gelu.astype(BF)
        slope_up[:, cols] = (u * (cdf + a * pdf)).astype(BF)

    def second_norm():
        @pl.loop(0, D // 256)
        def _(t):
            cols = block(t, 256)
            w = wd[:, :, :, :, :, cols].reshape(FF, 256)
            acc[:, cols] = mm(zed[...], w) + smallf[pl.ds(BD, 1), cols]

        def step(i, sums):
            r = block(i, 64)
            h = acc[r, :] + y1[r, :]
            centre = h - row_mean(h)
            rs = lax.rsqrt(row_mean(centre * centre) + EPSILON)
            xh = centre * rs
            gain = smallf[pl.ds(G2, 1), :]
            valid = (lax.broadcasted_iota(jnp.int32, (64, D), 0) + i * 64) < len_s
            res = jnp.where(valid, xh * gain + smallf[pl.ds(B2, 1), :], 0.0).astype(BF)
            outv[pl.ds(i * 4, 4)] = res.reshape(4, 16, D)
            up = jnp.where(valid, gs[pl.ds(i * 4, 4)].reshape(64, D).astype(F32), 0.0)
            dx = up * gain
            dh = rs * (dx - row_mean(dx) - xh * row_mean(dx * xh))
            low = dh.astype(BF)
            acc[r, :] = dh
            dfb[r, :] = low
            sg, sb, sd = sums
            return (
                sg + jnp.sum(up * xh, axis=0, keepdims=True),
                sb + jnp.sum(up, axis=0, keepdims=True),
                sd + jnp.sum(low.astype(F32), axis=0, keepdims=True),
            )

        zero = jnp.zeros((1, D), F32)
        sg, sb, sd = lax.fori_loop(0, L // 64, step, (zero, zero, zero))
        sgrad[pl.ds(G2, 1), :] = sg
        sgrad[pl.ds(B2, 1), :] = sb
        sgrad[pl.ds(BD, 1), :] = sd

    def ff_back(i):
        cols = block(i, D)
        dz = mm_nt(dfb[...], wd[pl.ds(i * Z // 4, Z // 4)].reshape(D, D))
        dgate = (dz * slope_up[:, cols].astype(F32)).astype(BF)
        dup = (dz * act[:, cols].astype(F32)).astype(BF)
        act[:, cols] = dup
        acc[...] += mm_nt(dgate, w_all(4 + 2 * i)) + mm_nt(dup, w_all(5 + 2 * i))
        wa[4 + 2 * i] = mm(tr[...], dgate).astype(BF).reshape(w_pc)

    def ff_back_rest(i):
        cols = block(i, D)
        wa[5 + 2 * i] = mm(tr[...], act[:, cols]).astype(BF).reshape(w_pc)
        wd[pl.ds(i * Z // 4, Z // 4)] = mm_tn(zed[:, cols], dfb[...]).astype(BF).reshape((Z // 4,) + wd.shape[1:])

    def first_norm_back():
        def step(i, sums):
            r = block(i, 64)
            up = acc[r, :]
            xh = xhat[r, :]
            dx = up * smallf[pl.ds(G1, 1), :]
            dh = rstd[r, :][:, :1] * (dx - row_mean(dx) - xh * row_mean(dx * xh))
            low = dh.astype(BF)
            xhat[r, :] = dh
            dfb[r, :] = low
            sg, sb, sd = sums
            return (
                sg + jnp.sum(up * xh, axis=0, keepdims=True),
                sb + jnp.sum(up, axis=0, keepdims=True),
                sd + jnp.sum(low.astype(F32), axis=0, keepdims=True),
            )

        zero = jnp.zeros((1, D), F32)
        sg, sb, sd = lax.fori_loop(0, L // 64, step, (zero, zero, zero))
        sgrad[pl.ds(G1, 1), :] = sg
        sgrad[pl.ds(B1, 1), :] = sb
        sgrad[pl.ds(BO, 1), :] = sd

    def out_back():
        y1b[...] = mm_nt(dfb[...], w_all(3)).astype(BF)
        wa[3] = mm_tn(ctxt[...], dfb[...]).astype(BF).reshape(w_pc)

    def dqkv(p):
        return act.at[:, pl.ds(D * p, D)]

    def attend_back(j):
        cols = block(j, 128)
        lane = lax.broadcasted_iota(jnp.int32, (L, 128), 1)
        q2, k2, v2 = (qkv[i, :, cols] for i in range(3))
        do2 = y1b[:, cols]
        kt = k2.T
        dv = dk = None
        for q in range(L // 256):
            qr = pl.ds(256 * q, 256)
            qs = slice(256 * q, 256 * q + 256)
            parts = []
            for s in range(2):
                half = (lane < 64) if s == 0 else (lane >= 64)
                qm = jnp.where(half, q2, jnp.zeros_like(q2))[qs]
                dm = jnp.where(half, do2, jnp.zeros_like(do2))[qs]
                st = mm_nt(k2, qm) * (0.125 * LOG2E) - dist[:, qr] * slopes[2 * j + s]
                pr = jnp.exp2(st - lse[2 * j + s, :, qr])
                dp = mm_nt(v2, dm)
                ds = (pr * (dp - jnp.sum(pr * dp, axis=0, keepdims=True))).astype(BF)
                a, b = mm(pr.astype(BF), dm), mm(ds, qm)
                dv = a if dv is None else dv + a
                dk = b if dk is None else dk + b
                parts.append(mm(kt[64 * s : 64 * s + 64], ds))
            dqkv(0)[qr, cols] = (jnp.concatenate(parts, axis=0).T * 0.125).astype(BF)
        dqkv(1)[:, cols] = (dk * 0.125).astype(BF)
        dqkv(2)[:, cols] = dv.astype(BF)

    def weights_back(p):
        x = xs[...].reshape(L, D)
        d = dqkv(p)
        wa[p] = mm_tn(x, d[...]).astype(BF).reshape(w_pc)
        if p != 1:
            r = BQ if p == 0 else BV
            sgrad[pl.ds(r, 1), :] = jnp.sum(d[...].astype(F32), axis=0, keepdims=True)

    def tokens_back():
        @pl.loop(0, L // 128)
        def _(i):
            r = block(i, 128)
            v = xhat[r, :]
            for p in range(3):
                v = v + mm_nt(dqkv(p)[r, :], w_all(p))
            raw[pl.ds(i * 8, 8)] = v.astype(BF).reshape(8, 16, D)

    def split_small():
        sparts[...] = jnp.zeros_like(sparts)
        for d in range(pc.total):
            at = d % fsdp * rows
            sparts[d, :, pl.ds(0, rows)] = sgrad[:, pl.ds(at, rows)]

    def undeal():
        @pl.loop(0, pc.total)
        def _(k):
            m, n = k // fsdp, lax.rem(k, fsdp)

            def find(f, at):
                return jnp.where(order[m, f] == n, f, at)

            DX[k] = dxr[m * fsdp + lax.fori_loop(0, fsdp, find, 0)]

    def spread(ex, t, at):
        first, count = at
        if first <= t < first + count:
            ex.start(t - first, count)

    take_raw = pltpu.make_async_copy(tokens_in, raw, rsem)
    take_raw.start()
    pc.signal()
    small_own[...] = jnp.zeros_like(small_own)
    for i, ref in enumerate(small_in):
        small_own[pl.ds(i, 1), pl.ds(0, rows)] = ref[...].astype(F32)
    prepare()
    take_raw.wait()
    deal()
    pc.wait()

    me_small = small.at[pc.f]
    keep_small = pltpu.make_async_copy(small_own, me_small, esems[2].at[2])
    keep_small.start()

    @pl.loop(1, fsdp)
    def _(k):
        f = lax.rem(pc.f + k, fsdp)
        remote(small_own, me_small, esems[0].at[2], esems[1].at[2], (pc.x, f)).start()

    small_all = remote(
        small.at[pl.ds(0, fsdp - 1)], small.at[pl.ds(0, fsdp - 1)], esems[0].at[2], esems[1].at[2],
        pc.dev(c=1 - pc.c),
    )

    def begin():
        ex_x.wait()
        small_all.wait_recv()
        keep_small.wait()
        place_small()
        for p in range(3):
            project(p)

    tasks = [(2, begin)]
    tasks += [(2, functools.partial(attend, j)) for j in range(HEADS // 2)]
    tasks += [(3, first_sum), (3, first_norm)]
    tasks += [(5 + 2 * i, functools.partial(gated, i)) for i in range(FF // D)]
    there = -1

    units = len(GATHER_UNITS)
    finished = [max(u for u in range(units) if GATHER_UNITS[u][0] == p) for p in range(PIECES)]
    for t in range(units + CORE_AT):
        spread(ex_x, t, X_AT)
        spread(ex_g, t, G_AT)
        for u in range(units):
            if t == max(0, u - AHEAD):
                g.start(u)
        for h in range(1, Z):
            for u in range(units):
                if t == max(0, u - AHEAD) + h:
                    g.hop(u, h)
        if 0 <= t - ROW_AT < units:
            g.row(t - ROW_AT)
        if 0 <= t - PLANE_AT < units:
            g.plane(t - PLANE_AT)
        if 0 <= t - CORE_AT < units:
            u = t - CORE_AT
            g.core(u)
            there = max([p for p in range(PIECES) if finished[p] <= u], default=-1)
            left = units + CORE_AT - 1 - t
            if tasks and tasks[0][0] <= there:
                tasks.pop(0)[1]()
            while len(tasks) > left and tasks[0][0] <= there:
                tasks.pop(0)[1]()
    ex_g.wait()
    ex_x.done()
    second_norm()
    if O_FIRST:
        ex_o.start()
    pc.finish()

    units = len(SCATTER_UNITS)
    stages = STAGES if STAGES else (("core", 1), ("plane", 3), ("row", 5), ("middle", 6), ("line", 8), ("last", 10))
    for t in range(units + stages[-1][1]):
        if t < 8:
            (ff_back_rest if t % 2 else ff_back)(t // 2)
        if t == 8:
            first_norm_back()
            out_back()
        if 9 <= t < 12:
            pl.loop(2 * (t - 9), 2 * (t - 9) + 2)(attend_back)
        if t == 12:
            tokens_back()
            for p in range(3):
                weights_back(p)
            split_small()
            ex_s.start()
        if not O_FIRST:
            spread(ex_o, t, O_AT)
        spread(ex_d, t, D_AT)
        if t < units:
            sc.start(t)
        for name, off in stages:
            if 0 <= t - off < units:
                u = t - off
                if name == "last":
                    sc.last(u, out_of(SCATTER_UNITS[u][0]))
                else:
                    getattr(sc, name)(u)
    ex_s.wait()

    def add(i, v):
        return v + gsum[i]

    total = lax.fori_loop(1, pc.total, add, gsum[0])
    SMALLG[...] = total[:, :rows]
    ex_d.wait()
    undeal()
    ex_o.wait()
    for e in (ex_g, ex_o, ex_d, ex_s):
        e.done()
    small_all.wait_send()
    pc.finish()


def hand_over(*refs):
    src, small, dst, parts, through, sem = refs[:6], refs[6], refs[7:13], refs[13:21], refs[21:27], refs[27]
    take = [pltpu.make_async_copy(a, b, sem.at[0, k]) for k, (a, b) in enumerate(zip(src, through))]
    give = [pltpu.make_async_copy(a, b, sem.at[1, k]) for k, (a, b) in enumerate(zip(through, dst))]
    for c in take:
        c.start()
    for k, ref in enumerate(parts):
        ref[...] = small[pl.ds(k, 1), :]
    for a, b in zip(take, give):
        a.wait()
        b.start()
    for c in give:
        c.wait()


def per_device(
    tokens_in, out_grad, seq_lengths, order, w_qkv, bias_q, bias_v, w_out, bias_out, ln1_gain, ln1_bias, w_gate_up,
    w_down, bias_down, ln2_gain, ln2_bias,
):
    fsdp = lax.axis_size("fsdp")
    total = 2 * fsdp
    rows = w_out.shape[0]
    here = tokens_in.shape[2]
    L = here * total
    Z = fsdp // 4
    small = [v.reshape(1, rows) for v in (bias_q, bias_v, bias_out, ln1_gain, ln1_bias, bias_down, ln2_gain, ln2_bias)]
    slopes = jnp.array(slope_list(HEADS), F32) * LOG2E
    hbm = pl.BlockSpec(memory_space=pl.ANY)
    smem = pl.BlockSpec(memory_space=pltpu.SMEM)
    vmem = pl.BlockSpec(memory_space=pltpu.VMEM)
    S = jax.ShapeDtypeStruct
    T = pltpu.SemaphoreType.DMA
    V = pltpu.VMEM
    rows_of = (total, here, D)
    results = pl.pallas_call(
        functools.partial(layer_kernel, fsdp, rows),
        out_shape=[
            S(rows_of, BF), S(rows_of, BF), S((rows, 3 * D), F32), S((rows, D), F32), S((rows, 2 * FF), F32),
            S((4 * rows, D), F32), S((8, rows), F32),
        ],
        in_specs=[smem] * 3 + [hbm] * 2 + [vmem] * 8 + [hbm] * 4,
        out_specs=[hbm] + [vmem] * 6,
        scratch_shapes=[
            V((12, Z, 2, 2, rows, D), BF), V((Z, 2, 2, 4, rows, D), BF), V(rows_of, BF), V(rows_of, BF),
            V(rows_of, BF), V(rows_of, BF), V((fsdp, 8, 128), F32), V((8, 128), F32), V((8, D), F32), V((3, L, D), BF), V((L, L), F32),
            V((HEADS, 1, L), F32), V((L, D), BF), V((L, D), F32), V((L, D), BF), V((L, D), F32), V((L, 128), F32),
            V((L, FF), BF), V((L, FF), BF), V((L, FF), BF), V((L, D), F32), V((L, D), BF), V((D, L), BF),
            V(rows_of, BF), V((8, D), F32), V((total, 8, 128), F32), V((total, 8, 128), F32),
            *Scatter.buffers(Z, rows), *Gather.sems(Z), *Scatter.sems(), T((6,)), T((6,)), T((6,)), T,
        ],
        compiler_params=pltpu.CompilerParams(collective_id=0, has_side_effects=True, vmem_limit_bytes=VMEM_LIMIT),
        name="layer",
    )(order, seq_lengths, slopes, tokens_in.reshape(rows_of), out_grad.reshape(rows_of), *small, w_qkv, w_out, w_gate_up, w_down)
    output, input_grad, gq, gw, gg, gd, *mine = pl.pallas_call(
        hand_over,
        out_shape=[S(r.shape, r.dtype) for r in results[:6]] + [S((1, rows), F32)] * 8,
        in_specs=[hbm] * 6 + [vmem],
        out_specs=[hbm] * 6 + [vmem] * 8,
        scratch_shapes=[V(r.shape, r.dtype) for r in results[:6]] + [T((2, 6))],
        name="hand_over",
    )(*results)
    mine = [v.reshape(rows) for v in mine]
    return (
        output.reshape(tokens_in.shape), input_grad.reshape(tokens_in.shape), gq, mine[BQ], mine[BV], gw, mine[BO],
        mine[G1], mine[B1], gg, gd, mine[BD], mine[G2], mine[B2],
    )


def solution(mesh):
    fsdp = mesh.shape["fsdp"]
    rows = D // fsdp
    kernels = mesh.shape["ctx"] == M and fsdp == 16 and rows % 16 == 0
    return jax.shard_map(
        per_device if kernels else per_device_plain,
        mesh=mesh,
        in_specs=(
            P(None, None, ("ctx", "fsdp"), None),
            P(None, None, ("ctx", "fsdp"), None),
            P(),
            P(),
            P("fsdp", None),
            P("fsdp"),
            P("fsdp"),
            P("fsdp", None),
            P("fsdp"),
            P("fsdp"),
            P("fsdp"),
            P("fsdp", None),
            P("fsdp", None),
            P("fsdp"),
            P("fsdp"),
            P("fsdp"),
        ),
        out_specs=(
            P(None, None, ("ctx", "fsdp"), None),
            P(None, None, ("ctx", "fsdp"), None),
            P("fsdp", None),
            P("fsdp"),
            P("fsdp"),
            P("fsdp", None),
            P("fsdp"),
            P("fsdp"),
            P("fsdp"),
            P("fsdp", None),
            P("fsdp", None),
            P("fsdp"),
            P("fsdp"),
            P("fsdp"),
        ),
        check_vma=False,
    )
```

profile of v0, /device:TPU:0, one launch (start us, length us, event | category | flops | bytes accessed | tf_op | source)
XLA Modules:
  0.0 244.2 jit_solution(17619765672886622395)
XLA Ops:
  0.7 238.8 %layer.1 = (bf16[32,16,768]{2,1,0:T(8,128)(2,1)}, bf16[32,16,768]{2,1,0:T(8,128)(2,1)}, f32[48,2304]{1,0:T(8,128)}, f32[48,768]{1,0:T(8,128)}, f32[48,6144]{1,0:...) custom-call(s32[2,16]{1,0:T(2,128)} %order.1, s32[2,16]{1,0:T(2,128)} %lengths.1, f32[12]{0:T(128)} %constant.7.slopes, ...), custom_call_target="tpu_custom_call" | custom-call | tf_op jit(solution)/shard_map/layer/pallas_call | solution.py:1221
  239.5 4.5 %hand_over.1 = (bf16[32,16,768]{2,1,0:T(8,128)(2,1)}, bf16[32,16,768]{2,1,0:T(8,128)(2,1)}, f32[48,2304]{1,0:T(8,128)}, f32[48,768]{1,0:T(8,128)}, f32[48,6144]{...) custom-call(bf16[32,16,768]{2,1,0:T(8,128)(2,1)} %get-tuple-element., ...), custom_call_target="tpu_custom_call" | custom-call | tf_op jit(solution)/shard_map/hand_over/pallas_call | solution.py:1240
where the time goes:
time: 248 us; the launch traced here: 244 us
  Pallas kernels  243 us (98%)
    pallas_call x1, Pallas kernels, per_device(): pl.pallas_call(functools.partial(layer_kernel, fsdp, rows), out_shape=[S(...  239 us

commit v1 on v0

--- a/solution.py
+++ b/solution.py
@@ -347,17 +347,14 @@
     return [(p, 0, D, w)]
 
 
-def halves(p, w=128):
-    return [(p, 384 * i, 384, w) for i in range(2)]
-
-
-GATHER_UNITS = sum([whole(p, 384 if p in (6, 10) else 256) for p in range(PIECES)], [])
+GATHER_UNITS = sum([whole(p, 0 if p == 15 else 384 if p in (6, 10) else 256) for p in range(PIECES)], [])
 SCATTER_UNITS = sum([whole(p, 256 if i % 3 else 128) for i, p in enumerate([*range(4, 16), 3, 0, 1, 2])], [])
 STAGES = ()
-AHEAD = 0
+SETTLE = 4
+AHEAD = 1
 ROW_AT = 4
 PLANE_AT = 6
-CORE_AT = 8
+CORE_AT = 7
 X_AT = (0, 7)
 G_AT = (7, 9)
 O_AT = (0, 8)
@@ -395,6 +392,7 @@
         self.c = lax.rem(self.f, 2)
         self.me = self.x * fsdp + self.f
         self.pending = []
+        self.turn = 0
 
     def dev(self, x=None, z=None, y=None, c=None):
         x = self.x if x is None else x
@@ -434,15 +432,18 @@
             copy.start()
         else:
             pl.when(cond)(copy.start)
-        self.pending.append((cond, copy))
-
-    def finish(self):
-        for cond, copy in self.pending:
-            if cond is None:
+        self.pending.append((self.turn, cond, copy))
+
+    def finish(self, before=None):
+        left = []
+        for turn, cond, copy in self.pending:
+            if before is not None and turn >= before:
+                left.append((turn, cond, copy))
+            elif cond is None:
                 copy.wait_send()
             else:
                 pl.when(cond)(copy.wait_send)
-        self.pending = []
+        self.pending = left
 
 
 def remote(src, dst, send, recv, device):
@@ -966,11 +967,12 @@
         dgate = (dz * slope_up[:, cols].astype(F32)).astype(BF)
         dup = (dz * act[:, cols].astype(F32)).astype(BF)
         act[:, cols] = dup
-        acc[...] += mm_nt(dgate, w_all(4 + 2 * i)) + mm_nt(dup, w_all(5 + 2 * i))
+        acc[...] += mm_nt(dgate, w_all(4 + 2 * i))
         wa[4 + 2 * i] = mm(tr[...], dgate).astype(BF).reshape(w_pc)
 
     def ff_back_rest(i):
         cols = block(i, D)
+        acc[...] += mm_nt(act[:, cols], w_all(5 + 2 * i))
         wa[5 + 2 * i] = mm(tr[...], act[:, cols]).astype(BF).reshape(w_pc)
         wd[pl.ds(i * Z // 4, Z // 4)] = mm_tn(zed[:, cols], dfb[...]).astype(BF).reshape((Z // 4,) + wd.shape[1:])
 
@@ -1111,6 +1113,8 @@
     units = len(GATHER_UNITS)
     finished = [max(u for u in range(units) if GATHER_UNITS[u][0] == p) for p in range(PIECES)]
     for t in range(units + CORE_AT):
+        pc.turn = t
+        pc.finish(t - SETTLE)
         spread(ex_x, t, X_AT)
         spread(ex_g, t, G_AT)
         for u in range(units):
@@ -1143,6 +1147,8 @@
     units = len(SCATTER_UNITS)
     stages = STAGES if STAGES else (("core", 1), ("plane", 3), ("row", 5), ("middle", 6), ("line", 8), ("last", 10))
     for t in range(units + stages[-1][1]):
+        pc.turn = t
+        pc.finish(t - SETTLE)
         if t < 8:
             (ff_back_rest if t % 2 else ff_back)(t // 2)
         if t == 8:

time: 248 us -> 245 us (0.988)
  no operation moved by 1% of the time
where the time goes in v1:
time: 245 us; the launch traced here: 242 us
  Pallas kernels  241 us (98%)
    pallas_call x1, Pallas kernels, per_device(): pl.pallas_call(functools.partial(layer_kernel, fsdp, rows), out_shape=[S(...  237 us

profile of v1, /device:TPU:0, one launch (start us, length us, event | category | flops | bytes accessed | tf_op | source)
XLA Modules:
  0.0 241.9 jit_solution(12547298396274808761)
XLA Ops:
  0.7 236.5 %layer.1 = (bf16[32,16,768]{2,1,0:T(8,128)(2,1)}, bf16[32,16,768]{2,1,0:T(8,128)(2,1)}, f32[48,2304]{1,0:T(8,128)}, f32[48,768]{1,0:T(8,128)}, f32[48,6144]{1,0:...) custom-call(s32[2,16]{1,0:T(2,128)} %order.1, s32[2,16]{1,0:T(2,128)} %lengths.1, f32[12]{0:T(128)} %constant.7.slopes, ...), custom_call_target="tpu_custom_call" | custom-call | tf_op jit(solution)/shard_map/layer/pallas_call | solution.py:1227
  237.2 4.5 %hand_over.1 = (bf16[32,16,768]{2,1,0:T(8,128)(2,1)}, bf16[32,16,768]{2,1,0:T(8,128)(2,1)}, f32[48,2304]{1,0:T(8,128)}, f32[48,768]{1,0:T(8,128)}, f32[48,6144]{...) custom-call(bf16[32,16,768]{2,1,0:T(8,128)(2,1)} %get-tuple-element., ...), custom_call_target="tpu_custom_call" | custom-call | tf_op jit(solution)/shard_map/hand_over/pallas_call | solution.py:1246

commit v2 on v1

--- a/solution.py
+++ b/solution.py
@@ -348,7 +348,7 @@
 
 
 GATHER_UNITS = sum([whole(p, 0 if p == 15 else 384 if p in (6, 10) else 256) for p in range(PIECES)], [])
-SCATTER_UNITS = sum([whole(p, 256 if i % 3 else 128) for i, p in enumerate([*range(4, 16), 3, 0, 1, 2])], [])
+SCATTER_UNITS = sum([whole(p, 256 if i % 4 else 128) for i, p in enumerate([*range(4, 16), 3, 0, 1, 2])], [])
 STAGES = ()
 SETTLE = 4
 AHEAD = 1

time: 245 us -> 243 us (level)
  no operation moved by 1% of the time
where the time goes in v2:
time: 243 us; the launch traced here: 240 us
  Pallas kernels  239 us (98%)
    pallas_call x1, Pallas kernels, per_device(): pl.pallas_call(functools.partial(layer_kernel, fsdp, rows), out_shape=[S(...  234 us

profile of v2, /device:TPU:0, one launch (start us, length us, event | category | flops | bytes accessed | tf_op | source)
XLA Modules:
  0.0 239.7 jit_solution(8647443376181551277)
XLA Ops:
  0.7 234.3 %layer.1 = (bf16[32,16,768]{2,1,0:T(8,128)(2,1)}, bf16[32,16,768]{2,1,0:T(8,128)(2,1)}, f32[48,2304]{1,0:T(8,128)}, f32[48,768]{1,0:T(8,128)}, f32[48,6144]{1,0:...) custom-call(s32[2,16]{1,0:T(2,128)} %order.1, s32[2,16]{1,0:T(2,128)} %lengths.1, f32[12]{0:T(128)} %constant.7.slopes, ...), custom_call_target="tpu_custom_call" | custom-call | tf_op jit(solution)/shard_map/layer/pallas_call | solution.py:1227
  235.0 4.5 %hand_over.1 = (bf16[32,16,768]{2,1,0:T(8,128)(2,1)}, bf16[32,16,768]{2,1,0:T(8,128)(2,1)}, f32[48,2304]{1,0:T(8,128)}, f32[48,768]{1,0:T(8,128)}, f32[48,6144]{...) custom-call(bf16[32,16,768]{2,1,0:T(8,128)(2,1)} %get-tuple-element., ...), custom_call_target="tpu_custom_call" | custom-call | tf_op jit(solution)/shard_map/hand_over/pallas_call | solution.py:1246
